TPU v7x, 128 devices: a whole 4x4x4 slice. The times are simulated.
128 devices in a mesh: row: 8 (over y, core), col: 16 (over z, x).
Axes of the slice: x: 4, y: 4, z: 4, core: 2. Of those that a mesh axis runs over, the one named last changes fastest.
Arguments:
- user_factors: float32 [16384, 128], P('row'), may hold values from -6 to 6
- item_factors: float32 [131072, 128], P(('row', 'col')), may hold values from -0.015625 to 0.015625
- fetch_list: int32 [8, 16, 128, 1], P('row', 'col'), may hold values from 0 to 7
- tile_user: int32 [8, 16, 32], P('row', 'col'), may hold values from 0 to 15
- tile_slot: int32 [8, 16, 32], P('row', 'col'), may hold values from 0 to 127
- entry_row: int32 [8, 16, 32, 512], P('row', 'col'), may hold values from 0 to 127
- entry_col: int32 [8, 16, 32, 512], P('row', 'col'), may hold values from 0 to 127
- entry_count: int32 [8, 16, 32, 512], P('row', 'col'), may hold values from 1 to 8
- tile_count: int32 [8, 16], P('row', 'col'), may hold values from 4 to 32, as said below
Outputs:
- solved: float32 [16384, 128], P('row')
Inputs may be any that keep to these rules, and one draw needn't show every extreme that they name: `tile_count`: at least 4 tiles live on every device; some device has all 32 live in every draw.
All inputs are finite; a program needn't handle non-finite values.
Results may differ from a plain program's by a relative error of at most 0.0003.
Values sent between devices are 32-bit elements; how exact they have to be, the bound alone decides.
A program may use at most 128 MiB of HBM per device.

v0:
```python
import jax
import jax.numpy as jnp
from jax import lax
from jax.sharding import PartitionSpec as P

K = 128
BLOCK = 128
ITERS = 3
HIGHEST = lax.Precision.HIGHEST
CONFIDENCE_SCALE = 40.0
RIDGE = 0.5
EPSILON = 1e-06


def conjugate(iterate, residual, apply_full):
    direction = residual
    norm_now = jnp.sum(residual * residual, axis=1, keepdims=True)
    for iteration in range(ITERS):
        image = apply_full(direction)
        alpha = norm_now / (jnp.sum(direction * image, axis=1, keepdims=True) + EPSILON)
        iterate = iterate + alpha * direction
        residual = residual - alpha * image
        norm_next = jnp.sum(residual * residual, axis=1, keepdims=True)
        direction = residual + norm_next / (norm_now + EPSILON) * direction
        norm_now = norm_next
    return iterate


def shards(
    user_factors,
    item_factors,
    fetch_list,
    tile_user,
    tile_slot,
    entry_row,
    entry_col,
    entry_count,
    tile_count,
):
    user_rows = user_factors.shape[0]
    user_blocks = user_rows // BLOCK
    local_blocks = item_factors.reshape(-1, BLOCK, K)
    wanted = fetch_list[0, 0]
    peers = wanted.shape[0]
    width = wanted.shape[1]
    asked = lax.all_to_all(wanted, ("row", "col"), split_axis=0, concat_axis=0, tiled=True)
    served = jnp.take(local_blocks, asked.reshape(-1), axis=0).reshape(peers, width, BLOCK, K)
    fetched = lax.all_to_all(
        served, ("row", "col"), split_axis=0, concat_axis=0, tiled=True
    ).reshape(-1, BLOCK, K)
    gram = lax.psum(
        jnp.dot(
            item_factors.T, item_factors, precision=HIGHEST, preferred_element_type=jnp.float32
        ),
        ("row", "col"),
    )
    users = tile_user[0, 0]
    slot_ids = tile_slot[0, 0]
    tiles = users.shape[0]
    tile_index = jnp.arange(tiles, dtype=jnp.int32)
    alive = (tile_index < tile_count[0, 0]).astype(jnp.float32)
    excess = CONFIDENCE_SCALE * entry_count[0, 0].astype(jnp.float32)
    weight_fit = excess * alive[:, None]
    weight_rhs = (1.0 + excess) * alive[:, None]
    rows_in = entry_row[0, 0]
    cols_in = entry_col[0, 0]
    block_ids = jnp.arange(BLOCK, dtype=jnp.int32)
    row_onehot = (rows_in[:, :, None] == block_ids[None, None, :]).astype(jnp.float32)
    col_onehot = (cols_in[:, :, None] == block_ids[None, None, :]).astype(jnp.float32)
    dense_fit = jnp.einsum(
        "tnu,tni->tui", row_onehot * weight_fit[:, :, None], col_onehot, precision=HIGHEST
    )
    dense_rhs = jnp.einsum(
        "tnu,tni->tui", row_onehot * weight_rhs[:, :, None], col_onehot, precision=HIGHEST
    )
    item_tiles = jnp.take(fetched, slot_ids, axis=0)
    owner_onehot = (users[None, :] == jnp.arange(user_blocks, dtype=jnp.int32)[:, None]).astype(
        jnp.float32
    )

    def tile_terms(vector):
        picked_users = jnp.take(vector.reshape(user_blocks, BLOCK, K), users, axis=0)
        scores = jnp.einsum("tuk,tik->tui", picked_users, item_tiles, precision=HIGHEST)
        pulled = jnp.einsum("tui,tik->tuk", dense_fit * scores, item_tiles, precision=HIGHEST)
        return jnp.einsum("bt,tuk->buk", owner_onehot, pulled, precision=HIGHEST).reshape(
            user_rows, K
        )

    rhs_pulled = jnp.einsum("tui,tik->tuk", dense_rhs, item_tiles, precision=HIGHEST)
    rhs_local = jnp.einsum("bt,tuk->buk", owner_onehot, rhs_pulled, precision=HIGHEST).reshape(
        user_rows, K
    )

    def extra(vector):
        return (
            jnp.dot(vector, gram, precision=HIGHEST, preferred_element_type=jnp.float32)
            + RIDGE * vector
        )

    start_terms = rhs_local - tile_terms(user_factors)

    def apply_whole(vector):
        return lax.psum(tile_terms(vector), "col") + extra(vector)

    residual = lax.psum(start_terms, "col") - extra(user_factors)
    solved = conjugate(user_factors, residual, apply_whole)
    return solved


def solution(mesh):
    return jax.shard_map(
        shards,
        mesh=mesh,
        in_specs=(
            P("row", None),
            P(("row", "col"), None),
            P("row", "col", None, None),
            P("row", "col", None),
            P("row", "col", None),
            P("row", "col", None, None),
            P("row", "col", None, None),
            P("row", "col", None, None),
            P("row", "col"),
        ),
        out_specs=P("row", None),
        check_vma=False,
    )
```

profile of v0, /device:TPU:0, one launch (start us, length us, event | category | flops | bytes accessed | tf_op | source)
XLA Modules:
  0.0 695.5 jit_solution(1226374862709490610)
XLA Ops:
  7.4 20.4 %all_to_all.20 = s32[128,1,1]{2,1,0:T(1,128)S(1)} all-to-all(s32[128,1,1]{2,1,0:T(1,128)S(1)} %copy.50), channel_id=1, replica_groups=mesh['row'=8,'col'=16] {'row','col'}, dimensions={0} | all-to-all | bytes 1024 | tf_op jit(solution)/shard_map/all_to_all | solution.py:46
  30.2 4.3 gather_fusion
  34.5 7.2 %bitcast_select_fusion = f32[128,1,128,128]{3,2,1,0:T(8,128)} fusion(f32[128,128,128]{2,1,0:T(8,128)} %gather_fusion, pred[128]{0:T(512)(128)(4,1)S(1)} %compare_and_fusion.1), kind=kLoop, calls=%fused_computation.6 | loop fusion | flops 2097152 | bytes 16777344 | tf_op jit(solution)/shard_map/jit(_take)/select_n | solution.py:47
  41.7 6.1 all-to-all-start.1
  52.4 8.1 %fusion = f32[32,128,128]{2,1,0:T(8,128)} fusion(f32[32,512]{1,0:T(8,128)S(1)} %get-tuple-element.11, s32[32,512]{1,0:T(8,128)S(1)} %bitcast.99, s32[32,512]{1,0:T(8,128)S(1)} %bitcast.101), kind=kOutput, calls=%fused_computation.7 | convolution fusion | flops 3227516928 | bytes 2293760 | tf_op jit(solution)/shard_map/tnu,tni->tui/dot_general | solution.py:70
  60.5 8.2 %fusion.2 = f32[32,128,128]{2,1,0:T(8,128)} fusion(s32[32,512]{1,0:T(8,128)S(1)} %bitcast.100, f32[32,512]{1,0:T(8,128)S(1)} %get-tuple-element.10, s32[32,512]{1,0:T(8,128)S(1)} %bitcast.102), kind=kOutput, calls=%fused_computation.10 | convolution fusion | flops 3227516928 | bytes 2293760 | tf_op jit(solution)/shard_map/tnu,tni->tui/dot_general | solution.py:73
  68.8 79.1 %all-to-all-done.1 = f32[128,1,128,128]{3,2,1,0:T(8,128)} async-done(((f32[128,1,128,128]{3,2,1,0:T(8,128)}), f32[128,1,128,128]{3,2,1,0:T(8,128)}, u32[]{:S(2)}, u32[]{:S(2)}) %all-to-all-start.1) | async-done | bytes 8388640 | tf_op jit(solution)/shard_map/all_to_all | solution.py:48
  147.9 4.1 gather_fusion.1
  152.0 3.9 fusion.50
  155.9 4.6 fusion.28
  168.4 2.6 copy.54
  172.3 81.8 %all-reduce.8.cloned.1.call-done = f32[128,128]{1,0:T(8,128)} async-done(((f32[128,128]{1,0:T(8,128)}), f32[128,128]{1,0:T(8,128)}) %all-reduce.8.cloned.1.call-update) | async-done | bytes 65552 | tf_op jit(solution)/shard_map/psum | solution.py:51
  254.1 90.1 %all-reduce.6.cloned.1.call-done = f32[2048,128]{0,1:T(8,128)} async-done(((f32[2048,128]{0,1:T(8,128)}), f32[2048,128]{0,1:T(8,128)}) %all-reduce.6.cloned.1.call-update) | async-done | bytes 1048592 | tf_op jit(solution)/shard_map/psum | solution.py:105
  344.2 3.0 fusion.13
  348.5 3.2 gather_fusion.3
  351.7 6.3 fusion.26
  358.0 3.6 fusion.34
  361.7 3.1 copy.69
  369.0 86.0 %all-reduce.10.cloned.1.call-done = f32[2048,128]{0,1:T(8,128)} async-done(((f32[2048,128]{0,1:T(8,128)}), f32[2048,128]{0,1:T(8,128)}) %all-reduce.10.cloned.1.call-update) | async-done | bytes 1048592 | tf_op jit(solution)/shard_map/psum | solution.py:103
  459.9 2.6 copy.79
  462.4 3.2 gather_fusion.4
  465.6 6.3 fusion.24
  472.0 3.6 fusion.32
  475.6 3.1 copy.72
  482.7 86.2 %all-reduce.12.cloned.1.call-done = f32[2048,128]{0,1:T(8,128)} async-done(((f32[2048,128]{0,1:T(8,128)}), f32[2048,128]{0,1:T(8,128)}) %all-reduce.12.cloned.1.call-update) | async-done | bytes 1048592 | tf_op jit(solution)/shard_map/psum | solution.py:103
  568.8 3.2 multiply_reduce_fusion.1
  576.1 3.2 gather_fusion.5
  579.3 6.3 fusion.22
  585.6 3.6 fusion.30
  593.8 86.4 %all-reduce.14.cloned.1.call-done = f32[2048,128]{0,1:T(8,128)} async-done(((f32[2048,128]{0,1:T(8,128)}), f32[2048,128]{0,1:T(8,128)}) %all-reduce.14.cloned.1.call-update) | async-done | bytes 1048592 | tf_op jit(solution)/shard_map/psum | solution.py:103
  680.2 3.0 fusion.41
  683.3 3.0 multiply_add_fusion
  (86 shorter events, 41.7 us)
Async XLA Ops:
  6.5 23.6 %copy-start = (f32[1024,128]{1,0:T(8,128)S(1)}, f32[1024,128]{1,0:T(8,128)}, u32[]{:S(2)}) copy-start(f32[1024,128]{1,0:T(8,128)} %param.12) | copy-start | bytes 1572868
  41.7 8.5 %copy-start.14 = (s32[1,1,32]{2,1,0:T(1,128)S(1)}, s32[1,1,32]{2,1,0:T(1,128)}, u32[]{:S(2)}) copy-start(s32[1,1,32]{2,1,0:T(1,128)} %param.14) | copy-start | bytes 388
  41.7 106.2 %all-to-all-start.1 = ((f32[128,1,128,128]{3,2,1,0:T(8,128)}), f32[128,1,128,128]{3,2,1,0:T(8,128)}, u32[]{:S(2)}, u32[]{:S(2)}) async-start(f32[128,1,128,128]{3,2,1,0:T(8,128)} %bitcast_select_fusion), calls=%async_computation.1 | async-start | bytes 16777216 | tf_op jit(solution)/shard_map/all_to_all | solution.py:48
  47.8 2.5 copy-start.10
  47.8 206.3 %all-reduce.8.cloned.1.call-start = ((), (), s32[]{:S(2)}) async-start(), calls=%async_computation.3 | async-start | bytes 131072 | tf_op jit(solution)/shard_map/psum | solution.py:51
  49.5 294.7 %all-reduce.6.cloned.1.call-start = ((), (), s32[]{:S(2)}) async-start(), calls=%async_computation.2 | async-start | bytes 2097152 | tf_op jit(solution)/shard_map/psum | solution.py:105
  50.2 2.0 copy-start.15
  50.3 2.1 copy-start.13
  50.3 2.2 copy-start.16
  50.3 2.2 copy-start.17
  151.9 4.0 copy-start.11
  155.9 4.6 copy-start.2
  171.0 284.0 %all-reduce.10.cloned.1.call-start = ((), (), s32[]{:S(2)}) async-start(), calls=%async_computation.4 | async-start | bytes 2097152 | tf_op jit(solution)/shard_map/psum | solution.py:103
  351.7 6.3 copy-start.3
  367.2 87.8 %copy-start.12 = (f32[128,128]{1,0:T(8,128)S(1)}, f32[128,128]{1,0:T(8,128)}, u32[]{:S(2)}) copy-start(f32[128,128]{1,0:T(8,128)} %all-reduce.8.cloned.1.call-done) | copy-start | bytes 196612
  368.5 200.3 %all-reduce.12.cloned.1.call-start = ((), (), s32[]{:S(2)}) async-start(), calls=%async_computation.5 | async-start | bytes 2097152 | tf_op jit(solution)/shard_map/psum | solution.py:103
  457.7 1.0 copy-start.8
  465.6 6.3 copy-start.4
  482.4 197.8 %all-reduce.14.cloned.1.call-start = ((), (), s32[]{:S(2)}) async-start(), calls=%async_computation.6 | async-start | bytes 2097152 | tf_op jit(solution)/shard_map/psum | solution.py:103
  568.8 3.3 copy-start.9
  568.8 3.5 copy-start.6
  579.3 6.3 copy-start.5
  593.8 89.5 %copy-start.7 = (f32[2048,128]{0,1:T(8,128)S(1)}, f32[2048,128]{0,1:T(8,128)}, u32[]{:S(2)}) copy-start(f32[2048,128]{0,1:T(8,128)} %multiply_add_fusion.2) | copy-start | bytes 3145732
  683.3 5.5 copy-start.1
Sparse Core Ops, SparseCore 0:
  53.4 200.6 all-reduce.7
  257.7 86.4 all-reduce.5
  368.7 86.2 all-reduce.9
  482.6 86.2 all-reduce.11
  593.9 86.2 all-reduce.13
where the time goes:
time: 702 us; the launch traced here: 696 us
  waiting for transfers between devices  510 us (73%)
  matrix products  80.1 us (11%)
  local copies, waits for them, and re-layouts  48.6 us (7%)
  blocking collectives  20.4 us (3%)
  other arithmetic  15.5 us (2%)
  between operations  14.4 us (2%)
    psum x3, waiting for transfers between devices, apply_whole(): return lax.psum(tile_terms(vector), 'col') + extra(vector)  259 us
    psum x1, waiting for transfers between devices, shards(): residual = lax.psum(start_terms, 'col') - extra(user_factors)  90.1 us
    psum x1, waiting for transfers between devices, shards(): lax.psum(jnp.dot(item_factors.T, item_factors, precision=HIGHEST, preferr...  81.8 us
    all_to_all x1, waiting for transfers between devices, shards(): lax.all_to_all(served, ('row', 'col'), split_axis=0, concat_axis=0, tiled...  79.1 us
    dot_general x4, matrix products, tile_terms(): jnp.einsum('tuk,tik->tui', picked_users, item_tiles, precision=HIGHEST)  23.5 us
    all_to_all x1, blocking collectives, shards(): lax.all_to_all(wanted, ('row', 'col'), split_axis=0, concat_axis=0, tiled...  20.4 us
  transfers between devices with their start and end apart: 6, of which 6 were waited for; matrix products, arithmetic and copies ran while one was open for 6% of the time, Pallas kernels for 0%

commit v1 on v0

--- a/solution.py
+++ b/solution.py
@@ -49,10 +49,13 @@
         served, ("row", "col"), split_axis=0, concat_axis=0, tiled=True
     ).reshape(-1, BLOCK, K)
     gram = lax.psum(
-        jnp.dot(
-            item_factors.T, item_factors, precision=HIGHEST, preferred_element_type=jnp.float32
+        lax.psum(
+            jnp.dot(
+                item_factors.T, item_factors, precision=HIGHEST, preferred_element_type=jnp.float32
+            ),
+            "row",
         ),
-        ("row", "col"),
+        "col",
     )
     users = tile_user[0, 0]
     slot_ids = tile_slot[0, 0]

time: 702 us -> 624 us (0.89)
  waiting for transfers between devices: 510 us -> 432 us
    psum x1, waiting for transfers between devices: 81.8 us -> 0.01 us  [shards(): lax.psum(jnp.dot(item_factors.T, item_factors, precision=HIGHEST, preferr...]
  transfers between devices with their start and end apart: 6 -> 6, of which waited for: 6 -> 5; matrix products, arithmetic and copies ran while one was open for 6% -> 7% of each run, Pallas kernels for 0% -> 0%
where the time goes in v1:
time: 624 us; the launch traced here: 618 us
  waiting for transfers between devices  432 us (69%)
  matrix products  80.2 us (13%)
  local copies, waits for them, and re-layouts  48.7 us (8%)
  blocking collectives  20.4 us (3%)
  other arithmetic  15.5 us (2%)
  between operations  14.4 us (2%)
  starting transfers between devices  6.85 us (1%)
    psum x3, waiting for transfers between devices, apply_whole(): return lax.psum(tile_terms(vector), 'col') + extra(vector)  259 us
    psum x1, waiting for transfers between devices, shards(): residual = lax.psum(start_terms, 'col') - extra(user_factors)  94 us
    all_to_all x1, waiting for transfers between devices, shards(): lax.all_to_all(served, ('row', 'col'), split_axis=0, concat_axis=0, tiled...  79 us
    dot_general x4, matrix products, tile_terms(): jnp.einsum('tuk,tik->tui', picked_users, item_tiles, precision=HIGHEST)  23.5 us
    all_to_all x1, blocking collectives, shards(): lax.all_to_all(wanted, ('row', 'col'), split_axis=0, concat_axis=0, tiled...  20.4 us
    dot_general x4, matrix products, tile_terms(): jnp.einsum('tui,tik->tuk', dense_fit * scores, item_tiles, precision=HIGH...  13.2 us
  transfers between devices with their start and end apart: 6, of which 5 were waited for; matrix products, arithmetic and copies ran while one was open for 7% of the time, Pallas kernels for 0%

profile of v1, /device:TPU:0, one launch (start us, length us, event | category | flops | bytes accessed | tf_op | source)
XLA Modules:
  0.0 617.8 jit_solution(16663239924551930547)
XLA Ops:
  7.4 20.4 %all_to_all.20 = s32[128,1,1]{2,1,0:T(1,128)S(1)} all-to-all(s32[128,1,1]{2,1,0:T(1,128)S(1)} %copy.50), channel_id=1, replica_groups=mesh['row'=8,'col'=16] {'row','col'}, dimensions={0} | all-to-all | bytes 1024 | tf_op jit(solution)/shard_map/all_to_all | solution.py:46
  30.2 4.3 gather_fusion
  34.5 7.2 %bitcast_select_fusion = f32[128,1,128,128]{3,2,1,0:T(8,128)} fusion(f32[128,128,128]{2,1,0:T(8,128)} %gather_fusion, pred[128]{0:T(512)(128)(4,1)S(1)} %compare_and_fusion.1), kind=kLoop, calls=%fused_computation.6 | loop fusion | flops 2097152 | bytes 16777344 | tf_op jit(solution)/shard_map/jit(_take)/select_n | solution.py:47
  41.7 6.1 all-to-all-start.1
  52.5 8.1 %fusion = f32[32,128,128]{2,1,0:T(8,128)} fusion(f32[32,512]{1,0:T(8,128)S(1)} %get-tuple-element.13, s32[32,512]{1,0:T(8,128)S(1)} %bitcast.99, s32[32,512]{1,0:T(8,128)S(1)} %bitcast.101), kind=kOutput, calls=%fused_computation.7 | convolution fusion | flops 3227516928 | bytes 2293760 | tf_op jit(solution)/shard_map/tnu,tni->tui/dot_general | solution.py:73
  60.6 8.2 %fusion.2 = f32[32,128,128]{2,1,0:T(8,128)} fusion(s32[32,512]{1,0:T(8,128)S(1)} %bitcast.100, f32[32,512]{1,0:T(8,128)S(1)} %get-tuple-element.12, s32[32,512]{1,0:T(8,128)S(1)} %bitcast.102), kind=kOutput, calls=%fused_computation.10 | convolution fusion | flops 3227516928 | bytes 2293760 | tf_op jit(solution)/shard_map/tnu,tni->tui/dot_general | solution.py:76
  68.8 79.0 %all-to-all-done.1 = f32[128,1,128,128]{3,2,1,0:T(8,128)} async-done(((f32[128,1,128,128]{3,2,1,0:T(8,128)}), f32[128,1,128,128]{3,2,1,0:T(8,128)}, u32[]{:S(2)}, u32[]{:S(2)}) %all-to-all-start.1) | async-done | bytes 8388640 | tf_op jit(solution)/shard_map/all_to_all | solution.py:48
  147.8 4.1 gather_fusion.1
  151.9 4.0 fusion.50
  155.9 4.6 fusion.28
  168.3 2.5 copy.54
  172.2 94.0 %all-reduce.15.cloned.1.call-done = (f32[2048,128]{0,1:T(8,128)}, f32[128,128]{1,0:T(8,128)}) async-done(((f32[2048,128]{0,1:T(8,128)}, f32[128,128]{1,0:T(8,128)}), (f32[2048,128]{0,1:T(8,128)}, f32[128,128]{1,0:T(8,128)})) %all-reduce.15.cloned.1.call-update) | async-done | bytes 1114128 | tf_op jit(solution)/shard_map/psum | solution.py:108
  266.3 3.0 fusion.13
  270.6 3.3 gather_fusion.3
  273.9 6.3 %fusion.26 = f32[32,128,128]{2,1,0:T(8,128)S(1)} fusion(f32[32,128,128]{2,1,0:T(8,128)} %gather_fusion.3, f32[32,128,128]{2,1,0:T(8,128)S(1)} %gather_fusion.1, pred[32]{0:T(512)(128)(4,1)S(1)} %get-tuple-element.17, pred[32]{0:T(512)(128)(4,1)S(1)} %get-tuple-element.18), kind=kOutput, calls=%fused_computation.39 | convolution fusion | flops 806354944 | bytes 6291520 | tf_op jit(solution)/shard_map/tuk,tik->tui/dot_general | solution.py:86
  280.2 3.6 fusion.34
  283.8 3.1 copy.69
  291.2 86.0 %all-reduce.9.cloned.1.call-done = f32[2048,128]{0,1:T(8,128)} async-done(((f32[2048,128]{0,1:T(8,128)}), f32[2048,128]{0,1:T(8,128)}) %all-reduce.9.cloned.1.call-update) | async-done | bytes 1048592 | tf_op jit(solution)/shard_map/psum | solution.py:106
  382.1 2.6 copy.79
  384.6 3.3 gather_fusion.4
  387.9 6.3 %fusion.24 = f32[32,128,128]{2,1,0:T(8,128)S(1)} fusion(f32[32,128,128]{2,1,0:T(8,128)} %gather_fusion.4, f32[32,128,128]{2,1,0:T(8,128)S(1)} %gather_fusion.1, pred[32]{0:T(512)(128)(4,1)S(1)} %get-tuple-element.17, pred[32]{0:T(512)(128)(4,1)S(1)} %get-tuple-element.18), kind=kOutput, calls=%fused_computation.37 | convolution fusion | flops 806354944 | bytes 6291520 | tf_op jit(solution)/shard_map/tuk,tik->tui/dot_general | solution.py:86
  394.2 3.6 fusion.32
  397.8 3.1 copy.72
  404.9 86.2 %all-reduce.11.cloned.1.call-done = f32[2048,128]{0,1:T(8,128)} async-done(((f32[2048,128]{0,1:T(8,128)}), f32[2048,128]{0,1:T(8,128)}) %all-reduce.11.cloned.1.call-update) | async-done | bytes 1048592 | tf_op jit(solution)/shard_map/psum | solution.py:106
  491.1 3.2 multiply_reduce_fusion.1
  495.9 2.5 copy.81
  498.4 3.3 gather_fusion.5
  501.7 6.3 %fusion.22 = f32[32,128,128]{2,1,0:T(8,128)S(1)} fusion(f32[32,128,128]{2,1,0:T(8,128)} %gather_fusion.5, f32[32,128,128]{2,1,0:T(8,128)S(1)} %gather_fusion.1, pred[32]{0:T(512)(128)(4,1)S(1)} %get-tuple-element.17, pred[32]{0:T(512)(128)(4,1)S(1)} %get-tuple-element.18), kind=kOutput, calls=%fused_computation.35 | convolution fusion | flops 806354944 | bytes 6291520 | tf_op jit(solution)/shard_map/tuk,tik->tui/dot_general | solution.py:86
  508.0 3.6 fusion.30
  516.1 86.4 %all-reduce.13.cloned.1.call-done = f32[2048,128]{0,1:T(8,128)} async-done(((f32[2048,128]{0,1:T(8,128)}), f32[2048,128]{0,1:T(8,128)}) %all-reduce.13.cloned.1.call-update) | async-done | bytes 1048592 | tf_op jit(solution)/shard_map/psum | solution.py:106
  602.5 3.0 fusion.41
  605.6 3.0 multiply_add_fusion
  (86 shorter events, 39.3 us)
Async XLA Ops:
  6.5 23.6 %copy-start = (f32[1024,128]{1,0:T(8,128)S(1)}, f32[1024,128]{1,0:T(8,128)}, u32[]{:S(2)}) copy-start(f32[1024,128]{1,0:T(8,128)} %param.12) | copy-start | bytes 1572868
  41.7 8.5 %copy-start.14 = (s32[1,1,32]{2,1,0:T(1,128)S(1)}, s32[1,1,32]{2,1,0:T(1,128)}, u32[]{:S(2)}) copy-start(s32[1,1,32]{2,1,0:T(1,128)} %param.14) | copy-start | bytes 388
  41.7 106.1 %all-to-all-start.1 = ((f32[128,1,128,128]{3,2,1,0:T(8,128)}), f32[128,1,128,128]{3,2,1,0:T(8,128)}, u32[]{:S(2)}, u32[]{:S(2)}) async-start(f32[128,1,128,128]{3,2,1,0:T(8,128)} %bitcast_select_fusion), calls=%async_computation.1 | async-start | bytes 16777216 | tf_op jit(solution)/shard_map/all_to_all | solution.py:48
  47.8 2.5 copy-start.10
  47.8 123.0 %all-reduce.7.cloned.1.call-start = ((), (), s32[]{:S(2)}) async-start(), calls=%async_computation.2 | async-start | bytes 131072 | tf_op jit(solution)/shard_map/psum | solution.py:52
  49.5 216.7 %all-reduce.15.cloned.1.call-start = ((), (), s32[]{:S(2)}) async-start(), calls=%async_computation.6 | async-start | bytes 2228224 | tf_op jit(solution)/shard_map/psum | solution.py:108
  50.3 2.0 copy-start.15
  50.3 2.1 copy-start.13
  50.3 2.2 copy-start.16
  50.3 2.2 copy-start.17
  151.9 4.0 copy-start.11
  155.9 4.6 copy-start.2
  170.9 206.3 %all-reduce.9.cloned.1.call-start = ((), (), s32[]{:S(2)}) async-start(), calls=%async_computation.3 | async-start | bytes 2097152 | tf_op jit(solution)/shard_map/psum | solution.py:106
  273.9 6.3 %copy-start.3 = (f32[32,128,128]{2,1,0:T(8,128)S(1)}, f32[32,128,128]{2,1,0:T(8,128)}, u32[]{:S(2)}) copy-start(f32[32,128,128]{2,1,0:T(8,128)} %fusion) | copy-start | bytes 6291460
  289.3 87.8 %copy-start.12 = (f32[128,128]{1,0:T(8,128)S(1)}, f32[128,128]{1,0:T(8,128)}, u32[]{:S(2)}) copy-start(f32[128,128]{1,0:T(8,128)} %get-tuple-element.9) | copy-start | bytes 196612
  290.8 200.4 %all-reduce.11.cloned.1.call-start = ((), (), s32[]{:S(2)}) async-start(), calls=%async_computation.4 | async-start | bytes 2097152 | tf_op jit(solution)/shard_map/psum | solution.py:106
  379.9 1.0 copy-start.8
  387.9 6.3 %copy-start.4 = (f32[32,128,128]{2,1,0:T(8,128)S(1)}, f32[32,128,128]{2,1,0:T(8,128)}, u32[]{:S(2)}) copy-start(f32[32,128,128]{2,1,0:T(8,128)} %fusion) | copy-start | bytes 6291460
  404.7 197.8 %all-reduce.13.cloned.1.call-start = ((), (), s32[]{:S(2)}) async-start(), calls=%async_computation.5 | async-start | bytes 2097152 | tf_op jit(solution)/shard_map/psum | solution.py:106
  491.1 3.3 copy-start.9
  491.1 3.5 copy-start.6
  501.7 6.3 %copy-start.5 = (f32[32,128,128]{2,1,0:T(8,128)S(1)}, f32[32,128,128]{2,1,0:T(8,128)}, u32[]{:S(2)}) copy-start(f32[32,128,128]{2,1,0:T(8,128)} %fusion) | copy-start | bytes 6291460
  516.1 89.5 %copy-start.7 = (f32[2048,128]{0,1:T(8,128)S(1)}, f32[2048,128]{0,1:T(8,128)}, u32[]{:S(2)}) copy-start(f32[2048,128]{0,1:T(8,128)} %multiply_add_fusion.2) | copy-start | bytes 3145732
  605.6 5.5 copy-start.1
Sparse Core Ops, SparseCore 0:
  51.0 109.0 all-reduce.6
  171.0 95.2 all-reduce.14
  290.9 86.2 all-reduce.8
  404.8 86.2 all-reduce.10
  516.3 86.2 all-reduce.12
